TPU v7x, 32 devices: a whole 2x2x4 slice. The times are simulated.
32 devices in a mesh: dp: 4 (over y, x), fsdp: 8 (over z, core).
Axes of the slice: x: 2, y: 2, z: 4, core: 2. Of those that a mesh axis runs over, the one named last changes fastest.
Arguments:
- tokens: bfloat16 [1152, 77, 512], P(('dp', 'fsdp')), may hold values from -6 to 6
- segment_ids: int32 [1152, 77], P(('dp', 'fsdp')), may hold values from 0 to 3, never falling along the last dimension, each value on 1 to 40 neighbouring positions
- qkv_weight: bfloat16 [786432], P(('dp', 'fsdp')), may hold values from -0.25 to 0.25
- out_weight: bfloat16 [262144], P(('dp', 'fsdp')), may hold values from -0.75 to 0.75
- up_weight: bfloat16 [1048576], P(('dp', 'fsdp')), may hold values from -0.25 to 0.25
- up_bias: bfloat16 [2048], P(('dp', 'fsdp')), may hold values from -1.75 to 1.75
- down_weight: bfloat16 [1048576], P(('dp', 'fsdp')), may hold values from -0.125 to 0.125
- small_params: bfloat16 [4096], P(('dp', 'fsdp'))
- cotangent: bfloat16 [1152, 77, 512], P(('dp', 'fsdp')), may hold values from -6 to 6
Outputs:
- block_output: bfloat16 [1152, 77, 512], P(('dp', 'fsdp'))
- grad_tokens: bfloat16 [1152, 77, 512], P(('dp', 'fsdp'))
- grad_qkv_weight: float32 [786432], P(('dp', 'fsdp'))
- grad_out_weight: float32 [262144], P(('dp', 'fsdp'))
- grad_up_weight: float32 [1048576], P(('dp', 'fsdp'))
- grad_up_bias: float32 [2048], P(('dp', 'fsdp'))
- grad_down_weight: float32 [1048576], P(('dp', 'fsdp'))
- grad_small: float32 [4096], P(('dp', 'fsdp'))
Inputs may be any that keep to these rules, and one draw needn't show every extreme that they name: `segment_ids`: along each packed row the ids never fall; each id labels one run of 1 to 40 consecutive tokens.
All inputs are finite; a program needn't handle non-finite values.
Results may differ from a plain program's by a relative error of at most 0.0091.
Values may be sent and summed in bfloat16 or wider, within the bound.
A program may use at most 192 MiB of HBM per device.

v0:
```python
import jax
import jax.numpy as jnp
from jax import lax
from jax.sharding import PartitionSpec as P

HEADS = 8
HEAD_DIM = 64
BLOCK_ROWS = 12


NORM_EPS = 1e-05
GELU_SLOPE = 1.702
MASKED_SCORE = -1e30


def norm_forward(values, norm_gain, norm_shift):
    center = jnp.mean(values, axis=-1, keepdims=True)
    centered = values - center
    inverse = lax.rsqrt(jnp.mean(centered * centered, axis=-1, keepdims=True) + NORM_EPS)
    normed = centered * inverse
    return (normed * norm_gain + norm_shift, normed, inverse)


def norm_backward(incoming, normed, inverse, norm_gain):
    scaled = incoming * norm_gain
    return inverse * (
        scaled
        - jnp.mean(scaled, axis=-1, keepdims=True)
        - normed * jnp.mean(scaled * normed, axis=-1, keepdims=True)
    )


def unpack(pieces, model_width, hidden):
    qkv_flat, out_flat, up_flat, bias_flat, down_flat, small_flat = pieces
    return (
        qkv_flat.reshape(model_width, 3 * model_width),
        out_flat.reshape(model_width, model_width),
        up_flat.reshape(model_width, hidden),
        bias_flat.astype(jnp.float32),
        down_flat.reshape(hidden, model_width),
        small_flat.reshape(8, model_width).astype(jnp.float32),
    )


def masked_scores(queries, key_rows, segments):
    places = jnp.arange(segments.shape[1])
    causal = places[None, :] <= places[:, None]
    allowed = (segments[:, :, None] == segments[:, None, :]) & causal[None]
    scores = jnp.einsum(
        "rqhd,rkhd->rhqk", queries, key_rows, preferred_element_type=jnp.float32
    ) * HEAD_DIM ** (-0.5)
    return jnp.where(allowed[:, None], scores, MASKED_SCORE)


def attend_forward(operands):
    queries, key_rows, value_rows, segments = operands
    masked = masked_scores(queries, key_rows, segments)
    highest = jnp.max(masked, axis=-1, keepdims=True)
    weights_exp = jnp.exp(masked - highest)
    row_total = jnp.sum(weights_exp, axis=-1, keepdims=True)
    prob_mat = weights_exp / row_total
    attended = jnp.einsum(
        "rhqk,rkhd->rqhd",
        prob_mat.astype(jnp.bfloat16),
        value_rows,
        preferred_element_type=jnp.float32,
    )
    return (attended, highest[..., 0] + jnp.log(row_total[..., 0]))


def attend_backward(operands):
    queries, key_rows, value_rows, segments, log_total, grad_attended = operands
    masked = masked_scores(queries, key_rows, segments)
    prob_mat = jnp.exp(masked - log_total[..., None])
    grad_values = jnp.einsum(
        "rhqk,rqhd->rkhd",
        prob_mat.astype(jnp.bfloat16),
        grad_attended,
        preferred_element_type=jnp.float32,
    )
    grad_probs = jnp.einsum(
        "rqhd,rkhd->rhqk", grad_attended, value_rows, preferred_element_type=jnp.float32
    )
    grad_scores = prob_mat * (grad_probs - jnp.sum(prob_mat * grad_probs, axis=-1, keepdims=True))
    scores_low = grad_scores.astype(jnp.bfloat16)
    grad_queries = jnp.einsum(
        "rhqk,rkhd->rqhd", scores_low, key_rows, preferred_element_type=jnp.float32
    ) * HEAD_DIM ** (-0.5)
    grad_keys = jnp.einsum(
        "rhqk,rqhd->rkhd", scores_low, queries, preferred_element_type=jnp.float32
    ) * HEAD_DIM ** (-0.5)
    return (grad_queries, grad_keys, grad_values)


def body(
    tokens,
    segment_ids,
    qkv_weight,
    out_weight,
    up_weight,
    up_bias,
    down_weight,
    small_params,
    cotangent,
):
    rows_local, seq_len, model_width = tokens.shape
    hidden = up_bias.shape[0] * lax.axis_size(("dp", "fsdp"))
    token_count = rows_local * seq_len
    block_count = rows_local // BLOCK_ROWS

    def split_heads(matrix):
        return matrix.reshape(block_count, BLOCK_ROWS, seq_len, HEADS, HEAD_DIM)

    def merge_heads(stacked):
        return stacked.reshape(token_count, model_width)

    gathered = (
        lax.all_gather(qkv_weight, ("dp", "fsdp"), axis=0, tiled=True),
        lax.all_gather(out_weight, ("dp", "fsdp"), axis=0, tiled=True),
        lax.all_gather(up_weight, ("dp", "fsdp"), axis=0, tiled=True),
        lax.all_gather(up_bias, ("dp", "fsdp"), axis=0, tiled=True),
        lax.all_gather(down_weight, ("dp", "fsdp"), axis=0, tiled=True),
        lax.all_gather(small_params, ("dp", "fsdp"), axis=0, tiled=True),
    )
    w_qkv, w_out, w_up, bias_up, w_down, small_vec = unpack(gathered, model_width, hidden)
    flat_rows = tokens.reshape(token_count, model_width).astype(jnp.float32)
    first_norm, normed_one, inverse_one = norm_forward(flat_rows, small_vec[0], small_vec[1])
    first_low = first_norm.astype(jnp.bfloat16)
    bias_qkv = jnp.concatenate([small_vec[2], jnp.zeros_like(small_vec[2]), small_vec[3]])
    qkv_low = (jnp.dot(first_low, w_qkv, preferred_element_type=jnp.float32) + bias_qkv).astype(
        jnp.bfloat16
    )
    queries = split_heads(qkv_low[:, :model_width])
    key_rows = split_heads(qkv_low[:, model_width : 2 * model_width])
    value_rows = split_heads(qkv_low[:, 2 * model_width :])
    segments = segment_ids.reshape(block_count, BLOCK_ROWS, seq_len)
    attended_heads, log_total = lax.map(attend_forward, (queries, key_rows, value_rows, segments))
    attended_low = merge_heads(attended_heads).astype(jnp.bfloat16)
    middle = (
        flat_rows + jnp.dot(attended_low, w_out, preferred_element_type=jnp.float32) + small_vec[4]
    )
    second_norm, normed_two, inverse_two = norm_forward(middle, small_vec[5], small_vec[6])
    second_low = second_norm.astype(jnp.bfloat16)
    pre_act = jnp.dot(second_low, w_up, preferred_element_type=jnp.float32) + bias_up
    gating = jax.nn.sigmoid(GELU_SLOPE * pre_act)
    act_low = (pre_act * gating).astype(jnp.bfloat16)
    result = middle + jnp.dot(act_low, w_down, preferred_element_type=jnp.float32) + small_vec[7]
    block_output = result.astype(jnp.bfloat16).reshape(tokens.shape)
    regathered = (
        lax.all_gather(qkv_weight, ("dp", "fsdp"), axis=0, tiled=True),
        lax.all_gather(out_weight, ("dp", "fsdp"), axis=0, tiled=True),
        lax.all_gather(up_weight, ("dp", "fsdp"), axis=0, tiled=True),
        lax.all_gather(up_bias, ("dp", "fsdp"), axis=0, tiled=True),
        lax.all_gather(down_weight, ("dp", "fsdp"), axis=0, tiled=True),
        lax.all_gather(small_params, ("dp", "fsdp"), axis=0, tiled=True),
    )
    w_qkv, w_out, w_up, bias_up, w_down, small_vec = unpack(regathered, model_width, hidden)
    upstream = cotangent.reshape(token_count, model_width).astype(jnp.float32)
    branch_low = upstream.astype(jnp.bfloat16)
    grad_down = jnp.einsum("tf,td->fd", act_low, branch_low, preferred_element_type=jnp.float32)
    grad_bias_down = jnp.sum(branch_low.astype(jnp.float32), axis=0)
    grad_act = jnp.einsum("td,fd->tf", branch_low, w_down, preferred_element_type=jnp.float32)
    pre_low = (grad_act * (gating + GELU_SLOPE * pre_act * gating * (1.0 - gating))).astype(
        jnp.bfloat16
    )
    grad_up = jnp.einsum("td,tf->df", second_low, pre_low, preferred_element_type=jnp.float32)
    grad_bias_up = jnp.sum(pre_low.astype(jnp.float32), axis=0)
    grad_norm_two = jnp.einsum("tf,df->td", pre_low, w_up, preferred_element_type=jnp.float32)
    grad_gain_two = jnp.sum(grad_norm_two * normed_two, axis=0)
    grad_shift_two = jnp.sum(grad_norm_two, axis=0)
    grad_middle = upstream + norm_backward(grad_norm_two, normed_two, inverse_two, small_vec[5])
    attn_low = grad_middle.astype(jnp.bfloat16)
    grad_out = jnp.einsum("td,te->de", attended_low, attn_low, preferred_element_type=jnp.float32)
    grad_bias_out = jnp.sum(attn_low.astype(jnp.float32), axis=0)
    grad_attended = jnp.einsum(
        "te,de->td", attn_low, w_out, preferred_element_type=jnp.float32
    ).astype(jnp.bfloat16)
    grad_queries, grad_keys, grad_values = lax.map(
        attend_backward,
        (queries, key_rows, value_rows, segments, log_total, split_heads(grad_attended)),
    )
    grad_qkv_low = jnp.concatenate(
        [merge_heads(grad_queries), merge_heads(grad_keys), merge_heads(grad_values)], axis=1
    ).astype(jnp.bfloat16)
    grad_qkv = jnp.einsum("td,te->de", first_low, grad_qkv_low, preferred_element_type=jnp.float32)
    column_sums = jnp.sum(grad_qkv_low.astype(jnp.float32), axis=0)
    grad_norm_one = jnp.einsum("te,de->td", grad_qkv_low, w_qkv, preferred_element_type=jnp.float32)
    grad_gain_one = jnp.sum(grad_norm_one * normed_one, axis=0)
    grad_shift_one = jnp.sum(grad_norm_one, axis=0)
    grad_input = grad_middle + norm_backward(grad_norm_one, normed_one, inverse_one, small_vec[0])
    grad_tokens = grad_input.astype(jnp.bfloat16).reshape(tokens.shape)
    grad_small_all = jnp.stack(
        [
            grad_gain_one,
            grad_shift_one,
            column_sums[:model_width],
            column_sums[2 * model_width :],
            grad_bias_out,
            grad_gain_two,
            grad_shift_two,
            grad_bias_down,
        ]
    ).reshape(-1)
    term_qkv = grad_qkv.reshape(-1)
    term_out = grad_out.reshape(-1)
    term_up = grad_up.reshape(-1)
    term_down = grad_down.reshape(-1)
    shares = (
        lax.psum_scatter(term_qkv, ("dp", "fsdp"), scatter_dimension=0, tiled=True),
        lax.psum_scatter(term_out, ("dp", "fsdp"), scatter_dimension=0, tiled=True),
        lax.psum_scatter(term_up, ("dp", "fsdp"), scatter_dimension=0, tiled=True),
        lax.psum_scatter(grad_bias_up, ("dp", "fsdp"), scatter_dimension=0, tiled=True),
        lax.psum_scatter(term_down, ("dp", "fsdp"), scatter_dimension=0, tiled=True),
        lax.psum_scatter(grad_small_all, ("dp", "fsdp"), scatter_dimension=0, tiled=True),
    )
    return (
        block_output,
        grad_tokens,
        shares[0],
        shares[1],
        shares[2],
        shares[3],
        shares[4],
        shares[5],
    )


def solution(mesh):
    in_specs = (
        P(("dp", "fsdp"), None, None),
        P(("dp", "fsdp"), None),
        P(("dp", "fsdp")),
        P(("dp", "fsdp")),
        P(("dp", "fsdp")),
        P(("dp", "fsdp")),
        P(("dp", "fsdp")),
        P(("dp", "fsdp")),
        P(("dp", "fsdp"), None, None),
    )
    out_specs = (
        P(("dp", "fsdp"), None, None),
        P(("dp", "fsdp"), None, None),
        P(("dp", "fsdp")),
        P(("dp", "fsdp")),
        P(("dp", "fsdp")),
        P(("dp", "fsdp")),
        P(("dp", "fsdp")),
        P(("dp", "fsdp")),
    )
    return jax.shard_map(body, mesh=mesh, in_specs=in_specs, out_specs=out_specs, check_vma=False)
```

profile of v0, /device:TPU:0, one launch (start us, length us, event | category | flops | bytes accessed | tf_op | source)
XLA Modules:
  0.0 791.8 jit_solution(17358783296036280019)
XLA Ops:
  25.3 43.0 %all-gather = bf16[32,1,128]{2,1,0:T(2,128)(2,1)S(1)} all-gather(bf16[1,1,128]{2,1,0:T(2,128)(2,1)S(1)} %bitcast.193), channel_id=1, replica_groups=mesh['dp'=4,'fsdp'=8] {'dp','fsdp'}, dimensions={0}, use_global_device_ids=true | all-gather | bytes 8448 | tf_op jit(solution)/shard_map/all_gather | solution.py:123
  75.8 41.9 %all_gather.25 = bf16[262144]{0:T(1024)(128)(2,1)} all-gather(bf16[8192]{0:T(1024)(128)(2,1)S(1)} %copy-done.18), channel_id=1, replica_groups=mesh['dp'=4,'fsdp'=8] {'dp','fsdp'}, dimensions={0}, use_global_device_ids=true | all-gather | bytes 540672 | tf_op jit(solution)/shard_map/all_gather | solution.py:119
  119.3 39.7 %all-reduce = bf16[2048]{0:T(1024)(128)(2,1)S(1)} all-reduce(bf16[2048]{0:T(1024)(128)(2,1)S(1)} %dynamic-update-slice), channel_id=1, replica_groups=mesh['dp'=4,'fsdp'=8] {'dp','fsdp'}, use_global_device_ids=true, to_apply=%add | all-reduce | flops 2048 | bytes 8192
  180.3 9.0 %copy.47 = bf16[3,12,77,8,64]{2,4,3,1,0:T(8,128)(2,1)} copy(bf16[3,12,77,8,64]{4,3,2,1,0:T(8,128)(2,1)} %reshape.249) | data formatting | bytes 5677056 | tf_op jit(solution)/shard_map/while | solution.py:137
  197.3 9.0 %copy.48 = bf16[3,12,77,8,64]{2,4,3,1,0:T(8,128)(2,1)} copy(bf16[3,12,77,8,64]{4,3,2,1,0:T(8,128)(2,1)} %reshape.251) | data formatting | bytes 5677056 | tf_op jit(solution)/shard_map/while | solution.py:137
  211.5 8.9 %copy.49 = bf16[3,12,77,8,64]{2,4,3,1,0:T(8,128)(2,1)} copy(bf16[3,12,77,8,64]{4,3,2,1,0:T(8,128)(2,1)} %reshape.252) | data formatting | bytes 5677056 | tf_op jit(solution)/shard_map/while | solution.py:137
  223.8 30.9 %while.26 = (s32[]{:T(128)}, bf16[3,12,77,8,64]{2,4,3,1,0:T(8,128)(2,1)}, f32[3,12,8,77]{3,2,1,0:T(8,128)}, bf16[3,12,77,8,64]{2,4,3,1,0:T(8,128)(2,1)}, s32[3,1...) while((s32[]{:T(128)}, ...), condition=%wide.region_5.6_spmd, body=%wide.region_2.5_spmd.sunk | while | flops 152682144 | bytes 42517128 | solution.py:137
  254.7 9.0 %copy.50 = bf16[3,12,77,8,64]{4,3,2,1,0:T(8,128)(2,1)} copy(bf16[3,12,77,8,64]{2,4,3,1,0:T(8,128)(2,1)} %get-tuple-element.100) | data formatting | bytes 5677056 | tf_op jit(solution)/shard_map/convert_element_type | solution.py:138
  283.4 18.6 %multiply_convert_fusion.2 = (bf16[2772,2048]{1,0:T(8,128)(2,1)}, f32[2772,2048]{1,0:T(8,128)}) fusion(f32[2048]{0:T(1024)S(1)} %convert_element_type.95, bf16[512,2048]{1,0:T(8,128)(2,1)} %reshape.254, f32[2772,512]{1,0:T(8,128)} %copy-done.2, f32[512]{0:T(512)S(1)} %bitcast.187, f32[512]{0:T(512)S(1)} %bitcast.177, f32[2772]{0:T(1024)S(1)} %add_rsqrt_fusion.1, ...), kind=kOutput, calls=%fused_computation.57 | convolution fusion | flops 5860141056 | bytes 41871008 | tf_op jit(solution)/shard_map/dot_general | solution.py:144
  306.3 22.3 %convert_reduce_fusion = (f32[2048]{0:T(1024)}, bf16[2772,2048]{1,0:T(8,128)(2,1)}) fusion(f32[2772,2048]{1,0:T(8,128)} %get-tuple-element.226, f32[2048]{0:T(1024)S(1)} %convert_element_type.95, bf16[2772,512]{1,0:T(8,128)(2,1)} %reshape.257, bf16[2048,512]{1,0:T(8,128)(2,1)} %reshape.255), kind=kOutput, calls=%fused_computation.55 | convolution fusion | flops 5887105024 | bytes 39014400 | tf_op jit(solution)/shard_map/td,fd->tf/dot_general | solution.py:162
  328.6 15.8 %multiply_reduce_fusion.2 = (f32[512]{0:T(512)}, f32[2772]{0:T(1024)S(1)}, f32[2772]{0:T(1024)S(1)}, f32[512]{0:T(512)}, f32[2772,512]{1,0:T(8,128)S(1)}) fusion(f32[2772,512]{1,0:T(8,128)} %copy-done.2, f32[2772]{0:T(1024)S(1)} %add_rsqrt_fusion.1, f32[2772]{0:T(1024)S(1)} %broadcast_multiply_fusion.5, f32[512]{0:T(512)S(1)} %bitcast.178, ...), kind=kOutput, calls=%fused_computation.64 | convolution fusion | flops 5826072576 | bytes 24855872 | tf_op jit(solution)/shard_map/tf,df->td/dot_general | solution.py:168
  344.4 13.0 %convolution_bitcast_fusion.1 = f32[64,16,8,128]{3,2,1,0:T(8,128)} fusion(bf16[2772,2048]{1,0:T(8,128)(2,1)} %get-tuple-element.230, f32[2772,512]{1,0:T(8,128)S(1)} %copy-done.3, f32[512]{0:T(512)S(1)} %bitcast.188, f32[512]{0:T(512)S(1)} %bitcast.179, f32[2772]{0:T(1024)S(1)} %add_rsqrt_fusion.1, f32[2772]{0:T(1024)S(1)} %broadcast_multiply_fusion.5), kind=kOutput, calls=%fused_computation.88 | convolution fusion | flops 5820401664 | bytes 21251744 | tf_op jit(solution)/shard_map/td,tf->df/dot_general | solution.py:166
  374.7 9.0 %copy.53 = bf16[3,12,77,8,64]{2,4,3,1,0:T(8,128)(2,1)} copy(bf16[3,12,77,8,64]{4,3,2,1,0:T(8,128)(2,1)} %reshape.258) | data formatting | bytes 5677056 | tf_op jit(solution)/shard_map/while | solution.py:178
  393.8 61.1 %while.27 = (s32[]{:T(128)}, bf16[3,12,77,8,64]{2,4,3,1,0:T(8,128)(2,1)}, bf16[3,12,77,8,64]{2,4,3,1,0:T(8,128)(2,1)}, bf16[3,12,77,8,64]{2,4,3,1,0:T(8,128)(2,1...) while((s32[]{:T(128)}, ...), condition=%wide.region_12.13_spmd, body=%wide.region_10.12_spmd.sunk | while | flops 370487424 | bytes 103597304 | solution.py:178
  455.0 8.9 %copy.55 = bf16[3,12,77,8,64]{4,3,2,1,0:T(8,128)(2,1)} copy(bf16[3,12,77,8,64]{2,4,3,1,0:T(8,128)(2,1)} %get-tuple-element.102) | data formatting | bytes 5677056 | tf_op jit(solution)/shard_map/convert.6
  473.5 8.9 %copy.56 = bf16[3,12,77,8,64]{4,3,2,1,0:T(8,128)(2,1)} copy(bf16[3,12,77,8,64]{2,4,3,1,0:T(8,128)(2,1)} %get-tuple-element.103) | data formatting | bytes 5677056 | tf_op jit(solution)/shard_map/convert.5
  489.8 9.0 %copy.57 = bf16[3,12,77,8,64]{4,3,2,1,0:T(8,128)(2,1)} copy(bf16[3,12,77,8,64]{2,4,3,1,0:T(8,128)(2,1)} %get-tuple-element.104) | data formatting | bytes 5677056 | tf_op jit(solution)/shard_map/convert.4
  498.8 8.4 %reshape.261 = bf16[2772,512]{1,0:T(8,128)(2,1)} reshape(bf16[3,12,77,8,64]{4,3,2,1,0:T(8,128)(2,1)} %copy.57) | data formatting | bytes 5677056 | tf_op jit(solution)/shard_map/reshape | solution.py:115
  517.2 10.1 %fusion.39 = f32[512,1536]{1,0:T(8,128)} fusion(bf16[2772,1536]{1,0:T(8,128)(2,1)} %constant_dynamic-update-slice_fusion, f32[2772,512]{1,0:T(8,128)S(1)} %bitcast.157, f32[512]{0:T(512)S(1)} %bitcast.175, f32[2772]{0:T(1024)S(1)} %copy-done.13, f32[512]{0:T(512)S(1)} %bitcast.170, f32[2772]{0:T(1024)S(1)} %copy-done.14), kind=kOutput, calls=%fused_computation.82 | convolution fusion | flops 4367075328 | bytes 17364640 | tf_op jit(solution)/shard_map/td,te->de/dot_general | solution.py:185
  534.3 9.1 %convolution_bitcast_fusion = f32[256,4,8,128]{3,2,1,0:T(8,128)S(1)} fusion(bf16[2772,2048]{1,0:T(8,128)(2,1)} %get-tuple-element.225, bf16[2772,512]{1,0:T(8,128)(2,1)S(1)} %copy-done.10), kind=kOutput, calls=%fused_computation.87 | convolution fusion | flops 5813305344 | bytes 18386944 | tf_op jit(solution)/shard_map/tf,td->fd/dot_general | solution.py:160
  551.3 12.2 %multiply_reduce_fusion.3 = (f32[512]{0:T(512)S(1)}, f32[2772]{0:T(1024)S(1)}, f32[2772]{0:T(1024)S(1)}, f32[512]{0:T(512)S(1)}, f32[2772,512]{1,0:T(8,128)}) fusion(f32[2772,512]{1,0:T(8,128)} %reshape.268, f32[2772]{0:T(1024)S(1)} %copy-done.13, f32[2772]{0:T(1024)S(1)} %copy-done.14, f32[512]{0:T(512)S(1)} %bitcast.171, ...), kind=kOutput, calls=%fused_computation.66 | convolution fusion | flops 4372746240 | bytes 21493056 | tf_op jit(solution)/shard_map/te,de->td/dot_general | solution.py:187
  573.9 10.5 %add_convert_fusion.4 = bf16[2772,512]{1,0:T(8,128)(2,1)S(1)} fusion(f32[2772,512]{1,0:T(8,128)} %copy-done.2, bf16[2772,2048]{1,0:T(8,128)(2,1)} %get-tuple-element.225, bf16[2048,512]{1,0:T(8,128)(2,1)} %reshape.255, f32[512]{0:T(512)S(1)} %bitcast.186), kind=kOutput, calls=%fused_computation.73 | convolution fusion | flops 5817563136 | bytes 21968896 | tf_op jit(solution)/shard_map/dot_general | solution.py:147
  587.4 40.6 %all-reduce.7 = (f32[2048]{0:T(1024)S(1)}, f32[4096]{0:T(1024)S(1)}) all-reduce(f32[2048]{0:T(1024)S(1)} %copy-done.23, f32[4096]{0:T(1024)S(1)} %bitcast.167), channel_id=5, replica_groups=mesh['dp'=4,'fsdp'=8] {'dp','fsdp'}, use_global_device_ids=true, to_apply=%region_19.20.clone | all-reduce | flops 6144 | bytes 49152
  629.2 149.8 %all-reduce.11.cloned.1.call-done = (f32[786432]{0:T(1024)}, f32[262144]{0:T(1024)}, f32[1048576]{0:T(1024)}, f32[1048576]{0:T(1024)}) async-done(((f32[786432]{0:T(1024)}, f32[262144]{0:T(1024)}, f32[1048576]{0:T(1024)}, f32[1048576]{0:T(1024)}), (f32[786432]{0:T(1024)}, f32[262144]{0:T(1024)}, f32[1048576]{0:T(1024)}, f32[1048576]{0:T(1024)})) %all-reduce.11.cloned.1.call-update) | async-done | bytes 12582928
  (252 shorter events, 269.8 us)
Async XLA Ops:
  7.2 151.8 %all-gather.5.cloned.1.call-start = ((), (), s32[]{:S(2)}) async-start(), calls=%async_computation | async-start | bytes 1622016 | tf_op jit(solution)/shard_map/all_gather | solution.py:118
  7.9 271.3 %all-gather.7.cloned.1.call-start = ((), (), s32[]{:S(2)}) async-start(), calls=%async_computation.1 | async-start | bytes 2162688 | tf_op jit(solution)/shard_map/all_gather | solution.py:120
  8.7 293.3 %all-gather.9.cloned.1.call-start = ((), (), s32[]{:S(2)}) async-start(), calls=%async_computation.2 | async-start | bytes 2162688 | tf_op jit(solution)/shard_map/all_gather | solution.py:122
  9.4 769.6 %all-reduce.11.cloned.1.call-start = ((), (), s32[]{:S(2)}) async-start(), calls=%async_computation.3 | async-start | bytes 25165824
  16.6 8.8 %copy-start.27 = (bf16[128]{0:T(256)(128)(2,1)S(1)}, bf16[128]{0:T(256)(128)(2,1)}, u32[]{:S(2)}) copy-start(bf16[128]{0:T(256)(128)(2,1)} %param.20) | copy-start | bytes 772
  68.9 6.8 copy-start.16
  68.9 6.8 copy-start.19
  69.7 6.1 copy-start.15
  69.7 6.1 copy-start.18
  72.0 47.0 %copy-start.28 = (bf16[64]{0:T(256)(128)(2,1)S(1)}, bf16[64]{0:T(256)(128)(2,1)}, u32[]{:S(2)}) copy-start(bf16[64]{0:T(256)(128)(2,1)} %param.18) | copy-start | bytes 388
  254.7 9.0 %copy-start.12 = (s32[3,12,77]{2,1,0:T(8,128)}, s32[3,12,77]{2,1,0:T(8,128)S(1)}, u32[]{:S(2)}) copy-start(s32[3,12,77]{2,1,0:T(8,128)S(1)} %get-tuple-element.424) | copy-start | bytes 33268
  328.6 15.8 %copy-start.3 = (f32[2772,512]{1,0:T(8,128)S(1)}, f32[2772,512]{1,0:T(8,128)}, u32[]{:S(2)}) copy-start(f32[2772,512]{1,0:T(8,128)} %copy-done.2) | copy-start | bytes 17031172
  344.4 13.0 %copy-start.9 = (bf16[2772,512]{1,0:T(8,128)(2,1)S(1)}, bf16[2772,512]{1,0:T(8,128)(2,1)}, u32[]{:S(2)}) copy-start(bf16[2772,512]{1,0:T(8,128)(2,1)} %reshape.257) | copy-start | bytes 8515588
  393.8 9.1 %slice-start.4 = ((s8[4718592]{0:T(1024)(128)(4,1)}), s8[4194304]{0:T(1024)(128)(4,1)S(1)}, s32[]{:S(2)}) async-start(s8[4718592]{0:T(1024)(128)(4,1)} %bitcast.160), calls=%async_computation.8 | async-start | bytes 8388608 | tf_op jit(solution)/shard_map/while
  399.1 5.7 slice-start.2
  414.2 9.1 %slice-start.4 = ((s8[4718592]{0:T(1024)(128)(4,1)}), s8[4194304]{0:T(1024)(128)(4,1)S(1)}, s32[]{:S(2)}) async-start(s8[4718592]{0:T(1024)(128)(4,1)} %bitcast.160), calls=%async_computation.8 | async-start | bytes 8388608 | tf_op jit(solution)/shard_map/while
  419.5 5.7 slice-start.2
  434.6 9.1 %slice-start.4 = ((s8[4718592]{0:T(1024)(128)(4,1)}), s8[4194304]{0:T(1024)(128)(4,1)S(1)}, s32[]{:S(2)}) async-start(s8[4718592]{0:T(1024)(128)(4,1)} %bitcast.160), calls=%async_computation.8 | async-start | bytes 8388608 | tf_op jit(solution)/shard_map/while
  507.2 9.9 %slice-start = ((s8[5685248]{0:T(1024)(128)(4,1)}), s8[4194304]{0:T(1024)(128)(4,1)S(1)}, s32[]{:S(2)}) async-start(s8[5685248]{0:T(1024)(128)(4,1)} %bitcast.156), calls=%async_computation.4 | async-start | bytes 8388608
  527.2 7.1 copy-start.10
  551.3 12.3 %copy-start.21 = (f32[512]{0:T(512)S(1)}, f32[512]{0:T(512)}, u32[]{:S(2)}) copy-start(f32[512]{0:T(512)} %convert_reduce_fusion.2) | copy-start | bytes 6148
  551.3 12.3 %copy-start.22 = (f32[512]{0:T(512)S(1)}, f32[512]{0:T(512)}, u32[]{:S(2)}) copy-start(f32[512]{0:T(512)} %get-tuple-element.204) | copy-start | bytes 6148
  551.3 12.3 %copy-start.25 = (f32[512]{0:T(512)S(1)}, f32[512]{0:T(512)}, u32[]{:S(2)}) copy-start(f32[512]{0:T(512)} %get-tuple-element.156) | copy-start | bytes 6148
  551.3 12.3 %copy-start.26 = (f32[512]{0:T(512)S(1)}, f32[512]{0:T(512)}, u32[]{:S(2)}) copy-start(f32[512]{0:T(512)} %get-tuple-element.162) | copy-start | bytes 6148
  (37 other events, 145.2 us)
Sparse Core Ops, SparseCore 0:
  11.0 57.8 all-gather.4
  71.9 55.7 all-gather.6
  130.6 55.4 all-gather.8
  546.6 232.3 all-reduce.10
where the time goes:
time: 801 us; the launch traced here: 792 us
  local copies, waits for them, and re-layouts  234 us (29%)
  matrix products  191 us (24%)
  blocking collectives  165 us (21%)
  waiting for transfers between devices  152 us (19%)
  other arithmetic  34.7 us (4%)
  between operations  14.4 us (2%)
    unnamed x5, waiting for transfers between devices  152 us
    unnamed x2, blocking collectives  80.3 us
    all_gather x1, blocking collectives, body(): lax.all_gather(small_params, ('dp', 'fsdp'), axis=0, tiled=True)  43 us
    all_gather x1, blocking collectives, body(): lax.all_gather(out_weight, ('dp', 'fsdp'), axis=0, tiled=True)  41.9 us
    another operation x7, local copies, waits for them, and re-layouts  40.4 us
    reshape x4, local copies, waits for them, and re-layouts, split_heads(): return matrix.reshape(block_count, BLOCK_ROWS, seq_len, HEADS, HEAD_DIM)  29.3 us
    while x3, local copies, waits for them, and re-layouts, body(): lax.map(attend_forward, (queries, key_rows, value_rows, segments))  26.9 us
    unnamed x68, local copies, waits for them, and re-layouts  25.5 us
  transfers between devices with their start and end apart: 4, of which 1 were waited for; matrix products, arithmetic and copies ran while one was open for 25% of the time, Pallas kernels for 0%

commit v1 on v0

v1 whole, which is shorter than its diff:
```python
import functools
import jax
import jax.numpy as jnp
from jax import lax
from jax.sharding import PartitionSpec as P
from jax.experimental import pallas as pl
from jax.experimental.pallas import tpu as pltpu
bf16=jnp.bfloat16; f32=jnp.float32
D=512; H=8; HD=64
NORM_EPS=1e-5; SLOPE=1.702
def nn(a,b): return lax.dot_general(a,b,(((1,),(0,)),((),())),preferred_element_type=f32)
def nt(a,b): return lax.dot_general(a,b,(((1,),(1,)),((),())),preferred_element_type=f32)
def tn(a,b): return lax.dot_general(a,b,(((0,),(0,)),((),())),preferred_element_type=f32)

def compute_kernel(R, S, SP, RB, FC, FF, phases,
    tok, seg, wqkv, wout, wup, bup, wdown, small, cot,
    out, gtok, gwqkv, gwout, gwup, gbup, gwdown, gsmall,
    xs, cs, FL, QKV, ATT, PT, GM, start, ost, osem, pre_s, ga_s, act_s, gp_s):
    NB=R//RB; M=RB*SP
    sm=small[...].astype(f32)
    g1,c1,bq,bv,bo,g2,c2,bd=[sm[i:i+1] for i in range(8)]
    xs[...]=jnp.zeros(xs.shape,f32)
    cs[...]=jnp.zeros(cs.shape,bf16)
    sg=seg[...]
    st=jnp.zeros(sg.shape,jnp.int32)
    for v in range(1,4):
        cnt=jnp.sum((sg<v).astype(f32),axis=1,keepdims=True).astype(jnp.int32)
        st=jnp.where(sg==v,cnt,st)
    st=jnp.concatenate([st,jnp.zeros((R,SP-S),jnp.int32)],axis=1)
    start[...]=jnp.concatenate([st]*4,axis=1).reshape(R,1,4*SP)

    def load_x(b):
        for i in range(RB):
            xs[SP*i:SP*i+S]=tok[b*RB+i].astype(f32)
    def norm(x):
        mean=jnp.sum(x,axis=-1,keepdims=True)*(1.0/D)
        xc=x-mean
        inv=lax.rsqrt(jnp.sum(xc*xc,axis=-1,keepdims=True)*(1.0/D)+NORM_EPS)
        return xc*inv, inv
    bqkv=jnp.concatenate([bq*0.125,jnp.zeros_like(bq),bv],axis=1)
    lane=lax.broadcasted_iota(jnp.int32,(1,256),1)
    hm=[(lane//HD==j).astype(f32).astype(bf16) for j in range(4)]
    low_half=lax.broadcasted_iota(jnp.int32,(1,128),1)<HD
    qi=lax.broadcasted_iota(jnp.int32,(SP,SP),1)
    def stack(v):
        return jnp.concatenate([v*hm[j] for j in range(4)],axis=0)
    def p1(b,_):
        load_x(b)
        n,_inv=norm(xs[...])
        fl=(n*g1+c1).astype(bf16)
        rows=pl.ds(pl.multiple_of(b*M,16),M)
        FL[rows]=fl
        QKV[rows,0:512]=(nn(fl,wqkv[:,0:512])*0.125+bqkv[:,0:512]).astype(bf16)
        QKV[rows,512:1536]=(nn(fl,wqkv[:,512:1536])+bqkv[:,512:1536]).astype(bf16)
        return _
    kidx=lax.broadcasted_iota(jnp.int32,(SP,4*SP),0)
    qidx=lax.broadcasted_iota(jnp.int32,(1,4*SP),1)
    qidx=qidx-SP*((qidx>=SP).astype(jnp.int32)+(qidx>=2*SP).astype(jnp.int32)+(qidx>=3*SP).astype(jnp.int32))
    def attn_row(r):
        rows=pl.ds(pl.multiple_of(r*SP,16),SP)
        allowed=(kidx>=start[r])&(kidx<=qidx)
        for g in range(2):
            q=QKV[rows,256*g:256*g+256]
            k=QKV[rows,512+256*g:512+256*g+256]
            s=nt(k,stack(q))
            s=jnp.where(allowed,s,-1e30)
            m=jnp.max(s,axis=0,keepdims=True)
            e=jnp.exp(s-m)
            p=(e*(1.0/jnp.sum(e,axis=0,keepdims=True))).astype(bf16)
            PT[2*r+g]=p
            pq=p.T
            for t in range(2):
                v=QKV[rows,1024+256*g+128*t:1024+256*g+128*t+128]
                o=nn(pq[2*SP*t:2*SP*t+2*SP],v)
                ATT[rows,256*g+128*t:256*g+128*t+128]=jnp.where(low_half,o[0:SP],o[SP:2*SP]).astype(bf16)
    UN=2
    def attn(r,_):
        for u in range(UN): attn_row(r*UN+u)
        return _
    def p2(b,_):
        load_x(b)
        for i in range(RB):
            cs[SP*i:SP*i+S]=cot[b*RB+i]
        rows=pl.ds(pl.multiple_of(b*M,16),M)
        att=ATT[rows]
        mid=xs[...]+nn(att,wout[...])+bo
        xh2,r2=norm(mid)
        second=(xh2*g2+c2).astype(bf16)
        branch=cs[...]
        acc=mid+bd
        gn2=jnp.zeros((M,D),f32)
        for c in range(FF//FC):
            cc=slice(c*FC,(c+1)*FC)
            pre=nn(second,wup[:,cc])+bup[:,cc].astype(f32)
            s=0.5*jnp.tanh((0.5*SLOPE)*pre)+0.5
            a=pre*s
            act=a.astype(bf16)
            ga=nt(branch,wdown[cc,:])
            gpf=ga*(s+SLOPE*a*(1.0-s))
            gp=gpf.astype(bf16)
            gbup[:,cc]+=jnp.sum(gp.astype(f32),axis=0,keepdims=True)
            acc=acc+nn(act,wdown[cc,:])
            gn2=gn2+nt(gp,wup[:,cc])
            gwdown[cc,:]+=tn(act,branch)
            gwup[:,cc]+=tn(second,gp)
        res=acc.astype(bf16)
        for i in range(RB):
            ost[i]=res[SP*i:SP*i+S]
        cp=pltpu.make_async_copy(ost,out.at[pl.ds(b*RB,RB)],osem)
        cp.start()
        h=gn2*g2
        m1=jnp.sum(h,axis=-1,keepdims=True)*(1.0/D)
        m2=jnp.sum(h*xh2,axis=-1,keepdims=True)*(1.0/D)
        bl=branch.astype(f32)
        gm=bl+r2*(h-m1-xh2*m2)
        GM[rows]=gm
        gl=gm.astype(bf16)
        gwout[...]+=tn(att,gl)
        ATT[rows]=nt(gl,wout[...]).astype(bf16)
        gsmall[4:5]+=jnp.sum(gl.astype(f32),axis=0,keepdims=True)
        gsmall[5:6]+=jnp.sum(gn2*xh2,axis=0,keepdims=True)
        gsmall[6:7]+=jnp.sum(gn2,axis=0,keepdims=True)
        gsmall[7:8]+=jnp.sum(bl,axis=0,keepdims=True)
        cp.wait()
        return _
    def battn_row(r):
        rows=pl.ds(pl.multiple_of(r*SP,16),SP)
        for g in range(2):
            go=ATT[rows,256*g:256*g+256]
            q=QKV[rows,256*g:256*g+256]
            v=QKV[rows,1024+256*g:1024+256*g+256]
            ps=PT[2*r+g]
            p=ps.astype(f32)
            bgo=stack(go)
            dp=nt(v,bgo)
            delta=jnp.sum(p*dp,axis=0,keepdims=True)
            ds=(p*(dp-delta)).astype(bf16)
            gv=nn(ps,bgo)
            gk=nn(ds,stack(q))
            dsq=ds.T
            gqs=[]
            for t in range(2):
                k=QKV[rows,512+256*g+128*t:512+256*g+128*t+128]
                o=nn(dsq[2*SP*t:2*SP*t+2*SP],k)
                gqs.append((jnp.where(low_half,o[0:SP],o[SP:2*SP])*0.125).astype(bf16))
            for t in range(2):
                QKV[rows,256*g+128*t:256*g+128*t+128]=gqs[t]
            QKV[rows,512+256*g:512+256*g+256]=gk.astype(bf16)
            QKV[rows,1024+256*g:1024+256*g+256]=gv.astype(bf16)
    def battn(r,_):
        for u in range(UN): battn_row(r*UN+u)
        return _
    def p3(b,_):
        load_x(b)
        rows=pl.ds(pl.multiple_of(b*M,16),M)
        gq=QKV[rows]
        gwqkv[...]+=tn(FL[rows],gq)
        gn1=nt(gq,wqkv[...])
        xh1,r1=norm(xs[...])
        h=gn1*g1
        m1=jnp.sum(h,axis=-1,keepdims=True)*(1.0/D)
        m2=jnp.sum(h*xh1,axis=-1,keepdims=True)*(1.0/D)
        res=(GM[rows]+r1*(h-m1-xh1*m2)).astype(bf16)
        for i in range(RB):
            ost[i]=res[SP*i:SP*i+S]
        cp=pltpu.make_async_copy(ost,gtok.at[pl.ds(b*RB,RB)],osem)
        cp.start()
        gsmall[0:1]+=jnp.sum(gn1*xh1,axis=0,keepdims=True)
        gsmall[1:2]+=jnp.sum(gn1,axis=0,keepdims=True)
        gsmall[2:3]+=jnp.sum(gq[:,0:512].astype(f32),axis=0,keepdims=True)
        gsmall[3:4]+=jnp.sum(gq[:,1024:1536].astype(f32),axis=0,keepdims=True)
        cp.wait()
        return _
    for ref in (gwqkv,gwout,gwup,gbup,gwdown,gsmall):
        ref[...]=jnp.zeros(ref.shape,f32)
    if '1' in phases: lax.fori_loop(0,NB,p1,0)
    if 'a' in phases: lax.fori_loop(0,R//UN,attn,0)
    if '2' in phases: lax.fori_loop(0,NB,p2,0)
    if 'b' in phases: lax.fori_loop(0,R//UN,battn,0)
    if '3' in phases: lax.fori_loop(0,NB,p3,0)

def compute(tok,seg,wqkv,wout,wup,bup,wdown,small,cot,RB=6,FC=512,phases='1a2b3'):
    R,S,_=tok.shape
    SP=(S+15)//16*16
    FF=wup.shape[1]
    M=RB*SP
    T=R*SP
    V=pltpu.VMEM
    vm=pl.BlockSpec(memory_space=pltpu.VMEM); an=pl.BlockSpec(memory_space=pl.ANY)
    outs=[jax.ShapeDtypeStruct(tok.shape,bf16),jax.ShapeDtypeStruct(tok.shape,bf16)]+[jax.ShapeDtypeStruct(s,f32) for s in ((D,3*D),(D,D),(D,FF),(1,FF),(FF,D),(8,D))]
    return pl.pallas_call(functools.partial(compute_kernel,R,S,SP,RB,FC,FF,phases),
        out_shape=outs, in_specs=[vm]*9, out_specs=[an]*2+[vm]*6,
        scratch_shapes=[V((M,D),f32),V((M,D),bf16),V((T,D),bf16),V((T,3*D),bf16),V((T,D),bf16),V((2*R,SP,4*SP),bf16),V((T,D),f32),V((R,1,4*SP),jnp.int32),V((RB,S,D),bf16),pltpu.SemaphoreType.DMA,
          V((8,128),f32),V((8,128),f32),V((8,128),bf16),V((8,128),bf16)],
        compiler_params=pltpu.CompilerParams(vmem_limit_bytes=60<<20),
    )(tok,seg,wqkv,wout,wup,bup,wdown,small,cot)


def body(tokens, segment_ids, qkv_weight, out_weight, up_weight, up_bias, down_weight, small_params, cotangent):
    axes = ("dp", "fsdp")
    gather = lambda v: lax.all_gather(v, axes, axis=0, tiled=True)
    scatter = lambda v: lax.psum_scatter(v.reshape(-1), axes, scatter_dimension=0, tiled=True)
    packed = lax.all_gather(jnp.concatenate([up_bias, small_params]), axes, axis=0, tiled=False)
    nb = up_bias.shape[0]
    bias = packed[:, :nb].reshape(1, -1)
    small = packed[:, nb:].reshape(8, D)
    FF = bias.shape[1]
    o = compute(tokens, segment_ids, gather(qkv_weight).reshape(D, 3 * D), gather(out_weight).reshape(D, D),
                gather(up_weight).reshape(D, FF), bias, gather(down_weight).reshape(FF, D), small, cotangent)
    return (o[0], o[1], scatter(o[2]), scatter(o[3]), scatter(o[4]), scatter(o[5]), scatter(o[6]), scatter(o[7]))


def solution(mesh):
    rows, flat = P(("dp", "fsdp"), None, None), P(("dp", "fsdp"))
    in_specs = (rows, P(("dp", "fsdp"), None), flat, flat, flat, flat, flat, flat, rows)
    out_specs = (rows, rows, flat, flat, flat, flat, flat, flat)
    return jax.shard_map(body, mesh=mesh, in_specs=in_specs, out_specs=out_specs, check_vma=False)
```

time: 801 us -> 585 us (0.73); the launches traced: 792 us -> 584 us
  local copies, waits for them, and re-layouts: 234 us -> 38.6 us
  matrix products: 191 us -> 0 us
  Pallas kernels: 0 us -> 134 us
  waiting for transfers between devices: 152 us -> 272 us
  blocking collectives: 165 us -> 125 us
  other arithmetic: 34.7 us -> 0.75 us
    dot_general x33 -> x0, matrix products: 191 us -> none  [the longest x1 22.3 us: body(): jnp.einsum('td,fd->tf', branch_low, w_down, preferred_element_type=jnp.fl...]
    pallas_call x0 -> x1, Pallas kernels: none -> 134 us  [compute(): pl.pallas_call(functools.partial(compute_kernel, R, S, SP, RB, FC, FF, ph...]
    all_gather x3, waiting for transfers between devices: 0.04 us -> 79.3 us  [body(): gather = lambda v: lax.all_gather(v, axes, axis=0, tiled=True)]
    reshape x16 -> x7, local copies, waits for them, and re-layouts: 82.5 us -> 19.6 us  [the longest x1 4.36 us: body(): gather(down_weight).reshape(FF, D)]
    while x64 -> x0, local copies, waits for them, and re-layouts: 49 us -> none  [the longest x3 26.9 us: body(): lax.map(attend_forward, (queries, key_rows, value_rows, segments))]
    all_gather x2 -> x1, blocking collectives: 84.9 us -> 43 us  [body(): gather = lambda v: lax.all_gather(v, axes, axis=0, tiled=True)]
    unnamed x5, waiting for transfers between devices: 152 us -> 192 us
    another operation x8 -> x0, local copies, waits for them, and re-layouts: 40.4 us -> none
  transfers between devices with their start and end apart: 4 -> 4, of which waited for: 1 -> 3; matrix products, arithmetic and copies ran while one was open for 25% -> 2% of each run, Pallas kernels for 0% -> 0%
where the time goes in v1:
time: 585 us; the launch traced here: 584 us
  waiting for transfers between devices  272 us (46%)
  Pallas kernels  134 us (23%)
  blocking collectives  125 us (21%)
  local copies, waits for them, and re-layouts  38.6 us (7%)
  between operations  13.8 us (2%)
    unnamed x5, waiting for transfers between devices  192 us
    pallas_call x1, Pallas kernels, compute(): pl.pallas_call(functools.partial(compute_kernel, R, S, SP, RB, FC, FF, ph...  134 us
    unnamed x2, blocking collectives  82.3 us
    all_gather x3, waiting for transfers between devices, body(): gather = lambda v: lax.all_gather(v, axes, axis=0, tiled=True)  79.3 us
    all_gather x1, blocking collectives, body(): gather = lambda v: lax.all_gather(v, axes, axis=0, tiled=True)  43 us
    unnamed x18, local copies, waits for them, and re-layouts  18.9 us
  transfers between devices with their start and end apart: 4, of which 3 were waited for; matrix products, arithmetic and copies ran while one was open for 2% of the time, Pallas kernels for 0%

profile of v1, /device:TPU:0, one launch (start us, length us, event | category | flops | bytes accessed | tf_op | source)
XLA Modules:
  0.0 584.3 jit_solution(11789931800408884864)
XLA Ops:
  7.9 0.7 all-gather.7.cloned.1.call-update
  8.7 0.7 all-gather.9.cloned.1.call-update
  9.4 0.7 pad_maximum_fusion
  10.4 42.2 %all-reduce = bf16[6144]{0:T(1024)(128)(2,1)S(1)} all-reduce(bf16[6144]{0:T(1024)(128)(2,1)S(1)} %dynamic-update-slice), channel_id=2, replica_groups=mesh['dp'=4,'fsdp'=8] {'dp','fsdp'}, use_global_device_ids=true, to_apply=%add | all-reduce | flops 6144 | bytes 24576
  52.7 0.7 reshape.55.bup
  54.0 43.0 %all_gather.19 = bf16[262144]{0:T(1024)(128)(2,1)S(1)} all-gather(bf16[8192]{0:T(1024)(128)(2,1)} %param.12), channel_id=1, replica_groups=mesh['dp'=4,'fsdp'=8] {'dp','fsdp'}, dimensions={0}, use_global_device_ids=true | all-gather | bytes 540672 | tf_op jit(solution)/shard_map/all_gather | solution.py:201
  97.0 1.1 reshape.53.wout
  98.1 4.3 reshape.52.wqkv
  102.4 25.1 %all-gather.7.cloned.1.call-done = bf16[1048576]{0:T(1024)(128)(2,1)} async-done(((bf16[32768]{0:T(1024)(128)(2,1)}), bf16[1048576]{0:T(1024)(128)(2,1)}) %all-gather.7.cloned.1.call-update) | async-done | bytes 2097168 | tf_op jit(solution)/shard_map/all_gather | solution.py:201
  127.5 4.2 reshape.54.wup
  131.6 54.2 %all-gather.9.cloned.1.call-done = bf16[1048576]{0:T(1024)(128)(2,1)} async-done(((bf16[32768]{0:T(1024)(128)(2,1)}), bf16[1048576]{0:T(1024)(128)(2,1)}) %all-gather.9.cloned.1.call-update) | async-done | bytes 2097168 | tf_op jit(solution)/shard_map/all_gather | solution.py:201
  185.8 4.4 reshape.56.wdown
  190.2 134.1 %shard_map.152 = (bf16[36,77,512]{2,1,0:T(8,128)(2,1)}, bf16[36,77,512]{2,1,0:T(8,128)(2,1)}, f32[512,1536]{1,0:T(8,128)}, f32[512,512]{1,0:T(8,128)}, f32[512,2...) custom-call(bf16[36,77,512]{2,1,0:T(8,128)(2,1)} %tok.1, s32[36,77]{1,0:T(8,128)} %seg.1, ...), custom_call_target="tpu_custom_call" | custom-call | tf_op jit(solution)/shard_map/pallas_call | solution.py:191
  324.3 2.5 copy.17
  326.8 4.4 reshape.58
  331.1 5.2 copy.18
  336.4 3.0 copy.19
  339.4 0.7 copy-done.1
  340.1 40.2 %all-reduce.7 = (f32[2048]{0:T(1024)S(1)}, f32[4096]{0:T(1024)S(1)}) all-reduce(f32[2048]{0:T(1024)S(1)} %bitcast.17, f32[4096]{0:T(1024)S(1)} %bitcast.15), channel_id=6, replica_groups=mesh['dp'=4,'fsdp'=8] {'dp','fsdp'}, use_global_device_ids=true, to_apply=%region_3.0.clone | all-reduce | flops 6144 | bytes 49152
  381.4 190.3 %all-reduce.11.cloned.1.call-done = (f32[786432]{0:T(1024)}, f32[262144]{0:T(1024)}, f32[1048576]{0:T(1024)}, f32[1048576]{0:T(1024)}) async-done(((f32[786432]{0:T(1024)}, f32[262144]{0:T(1024)}, f32[1048576]{0:T(1024)}, f32[1048576]{0:T(1024)}), (f32[786432]{0:T(1024)}, f32[262144]{0:T(1024)}, f32[1048576]{0:T(1024)}, f32[1048576]{0:T(1024)})) %all-reduce.11.cloned.1.call-update) | async-done | bytes 12582928
  571.7 1.6 dynamic-slice.2
  573.3 1.6 dynamic-slice.4
  574.9 1.5 dynamic-slice
  576.4 1.4 dynamic-slice.1
  (21 shorter events, 3.0 us)
Async XLA Ops:
  7.2 90.9 %all-gather.5.cloned.1.call-start = ((), (), s32[]{:S(2)}) async-start(), calls=%async_computation | async-start | bytes 1622016 | tf_op jit(solution)/shard_map/all_gather | solution.py:201
  7.9 119.6 %all-gather.7.cloned.1.call-start = ((), (), s32[]{:S(2)}) async-start(), calls=%async_computation.1 | async-start | bytes 2162688 | tf_op jit(solution)/shard_map/all_gather | solution.py:201
  8.7 177.2 %all-gather.9.cloned.1.call-start = ((), (), s32[]{:S(2)}) async-start(), calls=%async_computation.2 | async-start | bytes 2162688 | tf_op jit(solution)/shard_map/all_gather | solution.py:201
  9.4 562.3 %all-reduce.11.cloned.1.call-start = ((), (), s32[]{:S(2)}) async-start(), calls=%async_computation.3 | async-start | bytes 25165824
  331.1 5.2 copy-start
  339.4 0.7 copy-start.1
  339.4 0.7 copy-start.2
Sparse Core Ops, SparseCore 0:
  11.0 57.9 all-gather.4
  72.0 55.4 all-gather.6
  130.4 55.3 all-gather.8
  339.5 232.1 all-reduce.10

commit v2 on v1

v2 whole, which is shorter than its diff:
```python
import functools

import jax
import jax.numpy as jnp
from jax import lax
from jax.experimental import pallas as pl
from jax.experimental.pallas import tpu as pltpu
from jax.sharding import PartitionSpec as P

bf16 = jnp.bfloat16
f32 = jnp.float32
HEADS = 8
HEAD_DIM = 64
GROUP = 4
NORM_EPS = 1e-05
GELU_SLOPE = 1.702
MASKED_SCORE = -1e30
MESH = pl.DeviceIdType.MESH
ROW_BLOCK = 6
UNROLL = 2
ARRAYS = ("qkv", "out", "up", "down")


def nn(a, b):
    return lax.dot_general(a, b, (((1,), (0,)), ((), ())), preferred_element_type=f32)


def nt(a, b):
    return lax.dot_general(a, b, (((1,), (1,)), ((), ())), preferred_element_type=f32)


def tn(a, b):
    return lax.dot_general(a, b, (((0,), (0,)), ((), ())), preferred_element_type=f32)


def col_sum(v):
    return jnp.sum(v, axis=0, keepdims=True)


def lane_mean(v):
    return jnp.sum(v, axis=-1, keepdims=True) * (1.0 / v.shape[-1])


def normalize(x):
    xc = x - lane_mean(x)
    inv = lax.rsqrt(lane_mean(xc * xc) + NORM_EPS)
    return xc * inv, inv


def flip(index, bits):
    low, high = index % 2, index // 2
    if bits & 1:
        low = 1 - low
    if bits & 2:
        high = 1 - high
    return high * 2 + low


class Gather:
    def __init__(self, buf, send, recv, pos):
        self.buf, self.send, self.recv = buf, send, recv
        self.dp, self.z, self.c = pos

    def copy(self, index, slot, device):
        ref = self.buf.at[index]
        return pltpu.make_async_remote_copy(
            src_ref=ref, dst_ref=ref, send_sem=self.send.at[slot], recv_sem=self.recv.at[slot],
            device_id=device, device_id_type=MESH)

    def along_z(self, k, mine=True):
        z = self.z if mine else flip(self.z, k)
        return self.copy((self.dp, z, self.c), k - 1, (self.dp, flip(self.z, k) * 2 + self.c))

    def column(self, bit, mine=True):
        dp = self.dp if mine else flip(self.dp, bit)
        return self.copy((dp, slice(None), self.c), 2 + bit, (flip(self.dp, bit), self.z * 2 + self.c))

    def onward(self, bit, mine=True):
        other = 3 - bit
        dp = flip(self.dp, other) if mine else flip(self.dp, 3)
        half = pl.ds(0, 2) if bit == 2 else pl.ds(2, 2)
        return self.copy((dp, half, self.c), 4 + bit, (flip(self.dp, bit), self.z * 2 + self.c))

    def to_core(self, mine=True):
        c = self.c if mine else 1 - self.c
        return self.copy((slice(None), slice(None), c), 7, (self.dp, self.z * 2 + 1 - self.c))

    def start_z(self):
        for k in (1, 2, 3):
            self.along_z(k).start()

    def start_column(self):
        for k in (1, 2, 3):
            self.along_z(k, False).wait_recv()
        for bit in (1, 2):
            self.column(bit).start()

    def start_onward(self):
        for bit in (1, 2):
            self.column(3 - bit, False).wait_recv()
            self.onward(bit).start()

    def start_core(self):
        for bit in (1, 2):
            self.onward(bit, False).wait_recv()
        self.to_core().start()

    def finish(self):
        self.to_core(False).wait_recv()
        for k in (1, 2, 3):
            self.along_z(k).wait_send()
        for bit in (1, 2):
            self.column(bit).wait_send()
            self.onward(bit).wait_send()
        self.to_core().wait_send()


class Scatter:
    def __init__(self, grad, half, from_core, from_dp, from_z, send, recv, pos, dtype=bf16):
        self.grad, self.half, self.from_core, self.from_dp, self.from_z = grad, half, from_core, from_dp, from_z
        self.send, self.recv, self.dtype = send, recv, dtype
        self.dp, self.z, self.c = pos

    def copy(self, src, dst, slot, device):
        return pltpu.make_async_remote_copy(
            src_ref=src, dst_ref=dst, send_sem=self.send.at[slot], recv_sem=self.recv.at[slot],
            device_id=device, device_id_type=MESH)

    def core_copy(self):
        return self.copy(self.half, self.from_core, 0, (self.dp, self.z * 2 + 1 - self.c))

    def dp_copy(self, k):
        return self.copy(self.from_core.at[flip(self.dp, k)], self.from_dp.at[k - 1], k,
                         (flip(self.dp, k), self.z * 2 + self.c))

    def z_copy(self, k):
        return self.copy(self.from_dp.at[0, flip(self.z, k)], self.from_z.at[k - 1], 3 + k,
                         (self.dp, flip(self.z, k) * 2 + self.c))

    def start_core(self, whole=None):
        if whole is None:
            self.half[...] = self.grad[:, :, 1 - self.c].astype(self.dtype)
        else:
            zero, one = whole[:, :, 0], whole[:, :, 1]
            self.grad[...] = jnp.where(self.c == 0, zero, one)
            self.half[...] = jnp.where(self.c == 0, one, zero).astype(self.dtype)
        self.core_copy().start()

    def own(self, *index):
        return index if len(self.grad.shape) == 4 else index + (slice(None),) * (2 - len(index)) + (self.c,)

    def start_dp(self):
        self.core_copy().wait_recv()
        for k in (1, 2, 3):
            dp = flip(self.dp, k)
            self.from_core[dp] = (self.grad[self.own(dp)] + self.from_core[dp].astype(f32)).astype(self.dtype)
            self.dp_copy(k).start()

    def start_z(self):
        for k in (1, 2, 3):
            self.dp_copy(k).wait_recv()
        total = self.grad[self.own(self.dp)] + self.from_core[self.dp].astype(f32)
        for k in (1, 2, 3):
            total += self.from_dp[k - 1].astype(f32)
        self.grad[self.own(self.dp)] = total
        self.from_dp[0] = total.astype(self.dtype)
        for k in (1, 2, 3):
            self.z_copy(k).start()

    def finish(self):
        for k in (1, 2, 3):
            self.z_copy(k).wait_recv()
        total = self.grad[self.own(self.dp, self.z)]
        for k in (1, 2, 3):
            total += self.from_z[k - 1].astype(f32)
        self.core_copy().wait_send()
        for k in (1, 2, 3):
            self.dp_copy(k).wait_send()
            self.z_copy(k).wait_send()
        return total


def block_kernel(comm, R, S, SP, D, FF, *refs):
    RB, M, NB, FC = ROW_BLOCK, ROW_BLOCK * SP, R // ROW_BLOCK, FF // 4
    GW = GROUP * HEAD_DIM
    refs = list(refs)

    def take(n):
        out = refs[:n]
        del refs[:n]
        return out

    tok, seg, cot = take(3)
    shards = dict(zip(ARRAYS + ("small",), take(5)))
    out, gtok = take(2)
    if comm:
        shares = dict(zip(ARRAYS + ("small",), take(5)))
    else:
        grads = dict(zip(ARRAYS + ("small",), take(5)))
    tokv, cbuf, xs, cs, FL, QKV, ATT, PT, GM, start, bias, smallv, gbias, gsmall = take(14)
    tsem, csem, osem = take(3)
    if comm:
        weights = dict(zip(ARRAYS, take(4)))
        grads = dict(zip(ARRAYS + ("small",), take(5)))
        from_core = dict(zip(ARRAYS + ("small",), take(5)))
        from_dp = dict(zip(ARRAYS + ("small",), take(5)))
        from_z = dict(zip(ARRAYS + ("small",), take(5)))
        small_half, gsend, grecv, ssend, srecv = take(5)
    else:
        weights = {k: shards[k] for k in ARRAYS}

    tok_copy = pltpu.make_async_copy(tok, tokv, tsem)
    tok_copy.start()

    def cot_copy(b, slot):
        return pltpu.make_async_copy(cot.at[pl.ds(b * RB, RB)], cbuf.at[slot], csem.at[slot])

    def out_copy(b, slot):
        return pltpu.make_async_copy(cbuf.at[slot], out.at[pl.ds(b * RB, RB)], osem.at[slot])

    cot_copy(0, 0).start()

    if comm:
        dp = lax.axis_index("dp")
        fs = lax.axis_index("fsdp")
        pos = (dp, fs // 2, fs % 2)
        z, c = pos[1], pos[2]
        peers = [(flip(dp, k), fs) for k in (1, 2, 3)] + [(dp, flip(z, k) * 2 + c) for k in (1, 2, 3)]
        peers.append((dp, z * 2 + 1 - c))
        barrier = pltpu.get_barrier_semaphore()
        for peer in peers:
            pl.semaphore_signal(barrier, inc=1, device_id=peer, device_id_type=MESH)
        spread = grads["small"].reshape(256, 128)
        for name in ARRAYS:
            rows, cols = weights[name].shape[3:]
            if name == "qkv":
                cols -= 128
            per = cols // 128
            src = shards[name]
            spread[0 : src.shape[0]] = src[...].astype(f32)
            for j in range(per):
                weights[name][dp, z, c, :, 128 * j : 128 * j + 128] = spread[pl.ds(j, rows, stride=per), :].astype(bf16)
        weights["qkv"][dp, z, c, :, 3 * D :] = shards["small"][...]
        gathers = {n: Gather(weights[n], gsend.at[i], grecv.at[i], pos) for i, n in enumerate(ARRAYS)}
        pl.semaphore_wait(barrier, len(peers))
        gathers["qkv"].start_z()
        gathers["qkv"].start_column()
        for name in ARRAYS[1:]:
            gathers[name].start_z()
        rest = [gathers[n] for n in ARRAYS[1:]]

    xs[...] = jnp.zeros(xs.shape, f32)
    cs[...] = jnp.zeros(cs.shape, bf16)
    sg = seg[...]
    st = jnp.zeros(sg.shape, jnp.int32)
    for v in range(1, 4):
        count = jnp.sum((sg < v).astype(f32), axis=1, keepdims=True).astype(jnp.int32)
        st = jnp.where(sg == v, count, st)
    st = jnp.concatenate([st, jnp.zeros((R, SP - S), jnp.int32)], axis=1)
    start[...] = jnp.concatenate([st] * GROUP, axis=1).reshape(R, 1, GROUP * SP)
    for ref in (grads["out"], grads["up"], grads["down"], gbias, gsmall):
        ref[...] = jnp.zeros(ref.shape, f32)
    tok_copy.wait()

    def load_x(b):
        for i in range(RB):
            xs[SP * i : SP * i + S] = tokv[b * RB + i].astype(f32)

    def rows_of(b):
        return pl.ds(pl.multiple_of(b * M, 16), M)

    def norm_one(b, carry):
        load_x(b)
        GM[rows_of(b)] = normalize(xs[...])[0]
        return carry

    if comm:
        gathers["qkv"].start_onward()
        lax.fori_loop(0, NB // 2, norm_one, 0)
        gathers["qkv"].start_core()
        lax.fori_loop(NB // 2, NB, norm_one, 0)
        gathers["qkv"].finish()
        wq = weights["qkv"]
        for s in range(32):
            piece = wq[s // 8, (s % 8) // 2, s % 2, :, 3 * D :].astype(f32)
            smallv[s // 4 : s // 4 + 1, 128 * (s % 4) : 128 * (s % 4) + 128] = piece[0:1]
        for s in range(0, 32, 2):
            two = [wq[s // 8, (s % 8) // 2, i, :, 3 * D : 3 * D + 64].astype(f32)[1:2] for i in (0, 1)]
            bias[:, 64 * s : 64 * s + 128] = jnp.concatenate(two, axis=1)
        for g in rest:
            g.start_column()
    else:
        lax.fori_loop(0, NB, norm_one, 0)
        bias[...] = shards["small"][8:12].astype(f32).reshape(1, FF)
        smallv[...] = shards["small"][0:8].astype(f32)

    def w_qkv(a, b):
        return weights["qkv"][:, :, :, :, a:b].reshape(D, b - a)

    sm = smallv[...]
    g1, c1, bq, bv, bo, g2, c2, bd = [sm[i : i + 1] for i in range(8)]
    scale = HEAD_DIM ** (-0.5)
    bkv = jnp.concatenate([jnp.zeros_like(bv), bv], axis=1)
    lane = lax.broadcasted_iota(jnp.int32, (1, GW), 1)
    head_mask = [(lane // HEAD_DIM == j).astype(f32).astype(bf16) for j in range(GROUP)]
    low_half = lax.broadcasted_iota(jnp.int32, (1, 128), 1) < HEAD_DIM

    def stack(v):
        return jnp.concatenate([v * head_mask[j] for j in range(GROUP)], axis=0)

    def project(b, carry):
        rows = rows_of(b)
        fl = (GM[rows] * g1 + c1).astype(bf16)
        FL[rows] = fl
        QKV[rows, 0:D] = ((nn(fl, w_qkv(0, D)) + bq) * scale).astype(bf16)
        QKV[rows, D : 3 * D] = (nn(fl, w_qkv(D, 3 * D)) + bkv).astype(bf16)
        return carry

    kidx = lax.broadcasted_iota(jnp.int32, (SP, GROUP * SP), 0)
    qidx = lax.broadcasted_iota(jnp.int32, (1, GROUP * SP), 1)
    qidx = qidx - SP * sum((qidx >= SP * j).astype(jnp.int32) for j in range(1, GROUP))

    def attend_row(r):
        rows = pl.ds(pl.multiple_of(r * SP, 16), SP)
        allowed = (kidx >= start[r]) & (kidx <= qidx)
        for g in range(HEADS // GROUP):
            q = QKV[rows, GW * g : GW * g + GW]
            k = QKV[rows, D + GW * g : D + GW * g + GW]
            s = jnp.where(allowed, nt(k, stack(q)), MASKED_SCORE)
            e = jnp.exp(s - jnp.max(s, axis=0, keepdims=True))
            p = (e * (1.0 / col_sum(e))).astype(bf16)
            PT[2 * r + g] = p
            pq = p.T
            for t in range(GW // 128):
                at = GW * g + 128 * t
                v = QKV[rows, 2 * D + at : 2 * D + at + 128]
                o = nn(pq[2 * SP * t : 2 * SP * t + 2 * SP], v)
                ATT[rows, at : at + 128] = jnp.where(low_half, o[0:SP], o[SP : 2 * SP]).astype(bf16)

    def attend(i, carry):
        for u in range(UNROLL):
            attend_row(i * UNROLL + u)
        return carry

    def feed(b, carry):
        load_x(b)
        slot = b % 2
        cot_copy(b, slot).wait()

        for i in range(RB):
            cs[SP * i : SP * i + S] = cbuf[slot, i]

        @pl.when(b > 0)
        def _():
            out_copy(b - 1, 1 - slot).wait()

        @pl.when(b + 1 < NB)
        def _():
            cot_copy(b + 1, 1 - slot).start()

        rows = rows_of(b)
        att = ATT[rows]
        w_out = weights["out"][...].reshape(D, D)
        mid = xs[...] + nn(att, w_out) + bo
        GM[rows] = mid + bd
        xh2, r2 = normalize(mid)
        xs[...] = xh2
        second = (xh2 * g2 + c2).astype(bf16)
        branch = cs[...]
        gn2 = jnp.zeros((M, D), f32)
        for j in range(FF // FC):
            cc = slice(j * FC, (j + 1) * FC)
            w_up = weights["up"][:, :, :, :, cc].reshape(D, FC)
            w_down = weights["down"][j].reshape(FC, D)
            pre = nn(second, w_up) + bias[:, cc]
            s = 0.5 * jnp.tanh((0.5 * GELU_SLOPE) * pre) + 0.5
            a = pre * s
            act = a.astype(bf16)
            gp = (nt(branch, w_down) * (s + GELU_SLOPE * a * (1.0 - s))).astype(bf16)
            gbias[:, cc] += col_sum(gp.astype(f32))
            GM[rows] += nn(act, w_down)
            gn2 = gn2 + nt(gp, w_up)
            grads["down"][j] += tn(act, branch).reshape(grads["down"].shape[1:])
            grads["up"][:, :, :, :, cc] += tn(second, gp).reshape(grads["up"].shape[:4] + (FC,))
        res = GM[rows].astype(bf16)
        for i in range(RB):
            cbuf[slot, i] = res[SP * i : SP * i + S]
        out_copy(b, slot).start()
        xh2 = xs[...]
        h = gn2 * g2
        up = branch.astype(f32)
        gm = up + r2 * (h - lane_mean(h) - xh2 * lane_mean(h * xh2))
        GM[rows] = gm
        gl = gm.astype(bf16)
        grads["out"][...] += tn(att, gl).reshape(grads["out"].shape)
        ATT[rows] = nt(gl, w_out).astype(bf16)
        gsmall[4:5] += col_sum(gl.astype(f32))
        gsmall[5:6] += col_sum(gn2 * xh2)
        gsmall[6:7] += col_sum(gn2)
        gsmall[7:8] += col_sum(up)
        return carry

    def attend_back_row(r):
        rows = pl.ds(pl.multiple_of(r * SP, 16), SP)
        for g in range(HEADS // GROUP):
            here = slice(GW * g, GW * g + GW)
            q = QKV[rows, here]
            v = QKV[rows, 2 * D + GW * g : 2 * D + GW * g + GW]
            low = PT[2 * r + g]
            p = low.astype(f32)
            go = stack(ATT[rows, here])
            dpr = nt(v, go)
            ds = (p * (dpr - col_sum(p * dpr))).astype(bf16)
            gv = nn(low, go)
            gk = nn(ds, stack(q))
            dsq = ds.T
            parts = []
            for t in range(GW // 128):
                at = D + GW * g + 128 * t
                o = nn(dsq[2 * SP * t : 2 * SP * t + 2 * SP], QKV[rows, at : at + 128])
                parts.append((jnp.where(low_half, o[0:SP], o[SP : 2 * SP]) * scale).astype(bf16))
            for t in range(GW // 128):
                QKV[rows, GW * g + 128 * t : GW * g + 128 * t + 128] = parts[t]
            QKV[rows, D + GW * g : D + GW * g + GW] = gk.astype(bf16)
            QKV[rows, 2 * D + GW * g : 2 * D + GW * g + GW] = gv.astype(bf16)

    def attend_back(i, carry):
        for u in range(UNROLL):
            attend_back_row(i * UNROLL + u)
        return carry

    def input_grad(b, carry):
        load_x(b)
        rows = rows_of(b)
        gq = QKV[rows]
        gn1 = nt(gq, w_qkv(0, 3 * D))
        xh1, r1 = normalize(xs[...])
        h = gn1 * g1
        res = (GM[rows] + r1 * (h - lane_mean(h) - xh1 * lane_mean(h * xh1))).astype(bf16)
        for i in range(RB):
            tokv[b * RB + i] = res[SP * i : SP * i + S]
        gsmall[0:1] += col_sum(gn1 * xh1)
        gsmall[1:2] += col_sum(gn1)
        gsmall[2:3] += col_sum(gq[:, 0:D].astype(f32))
        gsmall[3:4] += col_sum(gq[:, 2 * D : 3 * D].astype(f32))
        return carry

    def loop(a, b, f):
        lax.fori_loop(a, b, f, 0)

    def qkv_grad(j):
        return tn(FL[...], QKV[:, j * D : (j + 1) * D]).reshape(4, 4, 2, D // 32, D)

    NA = R // UNROLL
    if not comm:
        loop(0, NB, project)
        loop(0, NA, attend)
        loop(0, NB, feed)
        out_copy(NB - 1, (NB - 1) % 2).wait()
        loop(0, NA, attend_back)
        for j in range(3):
            grads["qkv"][:, :, :, :, j * D : (j + 1) * D] = qkv_grad(j)
        loop(0, NB, input_grad)
        tok_back = pltpu.make_async_copy(tokv, gtok, tsem)
        tok_back.start()
        tok_back.wait()
        grads["small"][0:8] = gsmall[...]
        grads["small"][8:12] = gbias[...].reshape(4, D)
        return

    loop(0, NB, project)
    for g in rest:
        g.start_onward()
    loop(0, NA // 2, attend)
    for g in rest:
        g.start_core()
    loop(NA // 2, NA, attend)
    for g in rest:
        g.finish()
    loop(0, NB, feed)
    out_copy(NB - 1, (NB - 1) % 2).wait()

    scat = {}
    for i, name in enumerate(ARRAYS[1:]):
        scat[name] = Scatter(grads[name], weights[name].at[:, :, 0], from_core[name], from_dp[name], from_z[name],
                             ssend.at[i], srecv.at[i], pos)
    for j in range(3):
        cols = pl.ds(j * D, D)
        scat[j] = Scatter(grads["qkv"].at[:, :, :, cols], weights["up"].at[:, :, 1, :, cols],
                          from_core["qkv"].at[:, :, :, cols], from_dp["qkv"].at[:, :, :, cols],
                          from_z["qkv"].at[:, :, cols], ssend.at[3 + j], srecv.at[3 + j], pos)
    scat["small"] = Scatter(grads["small"], small_half, from_core["small"], from_dp["small"], from_z["small"],
                            ssend.at[6], srecv.at[6], pos, f32)
    rest = [scat[n] for n in ARRAYS[1:]]

    for s in rest:
        s.start_core()
    loop(0, NA // 3, attend_back)
    for s in rest:
        s.start_dp()
    loop(NA // 3, NA, attend_back)
    for j in range(3):
        scat[j].start_core(qkv_grad(j))
        if j:
            scat[j - 1].start_dp()
    for s in rest:
        s.start_z()
    loop(0, NB // 2, input_grad)
    scat[2].start_dp()
    for j in range(2):
        scat[j].start_z()
    loop(NB // 2, NB, input_grad)
    tok_back = pltpu.make_async_copy(tokv, gtok, tsem)
    tok_back.start()
    gs = grads["small"]
    for s in range(32):
        row = s // 4
        gs[s // 8, (s % 8) // 2, s % 2, 0:1, 0:128] = gsmall[row : row + 1, 128 * (s % 4) : 128 * (s % 4) + 128]
        two = gbias[:, 128 * (s // 2) : 128 * (s // 2) + 128]
        gs[s // 8, (s % 8) // 2, s % 2, 1:2, 0:64] = two[:, 64 * (s % 2) : 64 * (s % 2) + 64]
    small = scat["small"]
    small.start_core()
    scat[2].start_z()

    def give(name, total, first=0):
        rows, cols = total.shape
        per = shards[name].shape[0] // rows
        for j in range(cols // 128):
            shares[name][pl.ds(first + j, rows, stride=per), :] = total[:, 128 * j : 128 * j + 128]

    small.start_dp()
    for name in ARRAYS[1:]:
        give(name, scat[name].finish())
    small.start_z()
    for j in range(3):
        give("qkv", scat[j].finish(), j * D // 128)
    shares["small"][...] = small.finish()
    tok_back.wait()


def block_call(comm, tokens, segments, cotangent, pieces, FF):
    R, S, D = tokens.shape
    SP = (S + 15) // 16 * 16
    T, M = R * SP, ROW_BLOCK * SP
    V, dma = pltpu.VMEM, pltpu.SemaphoreType.DMA
    vm, hbm = pl.BlockSpec(memory_space=pltpu.VMEM), pl.BlockSpec(memory_space=pl.ANY)
    rows = {"qkv": (16, 3 * D), "out": (16, D), "up": (16, FF), "down": (FF // 32, D)}
    out_shape = [jax.ShapeDtypeStruct(tokens.shape, bf16)] * 2
    if comm:
        out_shape += [jax.ShapeDtypeStruct(p.shape, f32) for p in pieces[:4]]
        out_shape += [jax.ShapeDtypeStruct((8, 128), f32)]
    else:
        out_shape += [jax.ShapeDtypeStruct((4, 4, 2) + rows[n], f32) for n in ARRAYS]
        out_shape += [jax.ShapeDtypeStruct((12, D), f32)]
    scratch = [
        V((R, S, D), bf16), V((2, ROW_BLOCK, S, D), bf16), V((M, D), f32), V((M, D), bf16), V((T, D), bf16),
        V((T, 3 * D), bf16), V((T, D), bf16), V((2 * R, SP, GROUP * SP), bf16), V((T, D), f32),
        V((R, 1, GROUP * SP), jnp.int32), V((1, FF), f32), V((8, D), f32),
        V((1, FF), f32), V((8, D), f32), dma, dma((2,)), dma((2,)),
    ]
    if comm:
        small = {"small": (8, 128)}
        wide = {n: (r, cl + (128 if n == "qkv" else 0)) for n, (r, cl) in rows.items()}
        scratch += [V((4, 4, 2) + wide[n], bf16) for n in ARRAYS]
        for lead in ((4, 4, 2), (4, 4), (3, 4), (3,)):
            kind = f32 if lead == (4, 4, 2) else bf16
            scratch += [V(((4, 4) if n == "qkv" and kind == f32 else lead) + rows[n], kind) for n in ARRAYS]
            scratch += [V(lead + small["small"], f32)]
        scratch += [V((4, 4, 8, 128), f32), dma((4, 8)), dma((4, 8)), dma((7, 7)), dma((7, 7))]
    params = dict(vmem_limit_bytes=63 * 1000 * 1000 + 256 * 1024)
    if comm:
        params.update(collective_id=1, has_side_effects=True)
    return pl.pallas_call(
        functools.partial(block_kernel, comm, R, S, SP, D, FF),
        out_shape=out_shape,
        in_specs=[hbm, vm, hbm] + [vm] * 5,
        out_specs=[hbm, hbm] + [vm] * 5,
        scratch_shapes=scratch,
        compiler_params=pltpu.CompilerParams(**params),
    )(tokens, segments, cotangent, *pieces)


def body(sizes, tokens, segment_ids, qkv_weight, out_weight, up_weight, up_bias, down_weight, small_params, cotangent):
    D = tokens.shape[2]
    n = sizes[0] * sizes[1]
    FF = up_bias.shape[0] * n
    flats = (qkv_weight, out_weight, up_weight, down_weight)
    if sizes == (4, 8):
        tile = jnp.pad(jnp.concatenate([small_params, up_bias]), (0, 16 * 128 - 192)).reshape(16, 128)
        o = block_call(True, tokens, segment_ids, cotangent, [f.reshape(-1, 128) for f in flats] + [tile], FF)
        shares = [v.reshape(-1) for v in o[2:6]]
        return (o[0], o[1], shares[0], shares[1], shares[2], o[6][1, :64], shares[3], o[6][0])
    axes = ("dp", "fsdp")

    def gather(v):
        return lax.all_gather(v, axes, axis=0, tiled=True)

    def scatter(v):
        return lax.psum_scatter(v.reshape(-1), axes, scatter_dimension=0, tiled=True)

    packed = lax.all_gather(jnp.concatenate([small_params, up_bias]), axes, axis=0, tiled=False)
    count = small_params.shape[0]
    tile = jnp.concatenate([packed[:, :count].reshape(8, D), packed[:, count:].reshape(4, D)])
    whole = [gather(f) for f in flats]
    shapes = ((4, 4, 2, 16, 3 * D), (4, 4, 2, 16, D), (4, 4, 2, 16, FF), (4, 4, 2, FF // 32, D))
    o = block_call(False, tokens, segment_ids, cotangent, [w.reshape(s) for w, s in zip(whole, shapes)] + [tile], FF)
    return (o[0], o[1], scatter(o[2]), scatter(o[3]), scatter(o[4]), scatter(o[6][8:12]), scatter(o[5]), scatter(o[6][0:8]))


def solution(mesh):
    rows, flat = P(("dp", "fsdp"), None, None), P(("dp", "fsdp"))
    in_specs = (rows, P(("dp", "fsdp"), None), flat, flat, flat, flat, flat, flat, rows)
    out_specs = (rows, rows, flat, flat, flat, flat, flat, flat)
    sizes = (mesh.shape["dp"], mesh.shape["fsdp"])
    return jax.shard_map(functools.partial(body, sizes), mesh=mesh, in_specs=in_specs, out_specs=out_specs, check_vma=False)
```

time: 585 us -> 182 us (0.31)
  waiting for transfers between devices: 272 us -> 0 us
  blocking collectives: 125 us -> 0 us
  Pallas kernels: 134 us -> 170 us
  local copies, waits for them, and re-layouts: 38.6 us -> 10.4 us
  between operations: 13.8 us -> 0.66 us
    unnamed x5 -> x0, waiting for transfers between devices: 192 us -> none
    unnamed x2 -> x0, blocking collectives: 82.3 us -> none
    all_gather x3 -> x0, waiting for transfers between devices: 79.3 us -> none  [body(): gather = lambda v: lax.all_gather(v, axes, axis=0, tiled=True)]
    all_gather x1 -> x0, blocking collectives: 43 us -> none  [body(): gather = lambda v: lax.all_gather(v, axes, axis=0, tiled=True)]
    pallas_call x1, Pallas kernels: 134 us -> 170 us  [block_call(): pl.pallas_call(functools.partial(block_kernel, comm, R, S, SP, D, FF), ou...]
    reshape x7 -> x0, local copies, waits for them, and re-layouts: 19.6 us -> none  [the longest x1 4.36 us: body(): gather(down_weight).reshape(FF, D)]
    unnamed x18 -> x16, local copies, waits for them, and re-layouts: 18.9 us -> 8 us
  transfers between devices with their start and end apart: 4 -> 0, of which waited for: 3 -> 0; matrix products, arithmetic and copies ran while one was open for 2% -> 0% of each run, Pallas kernels for 0% -> 0%
where the time goes in v2:
time: 182 us
  Pallas kernels  170 us (93%)
  local copies, waits for them, and re-layouts  10.4 us (6%)
    pallas_call x1, Pallas kernels, block_call(): pl.pallas_call(functools.partial(block_kernel, comm, R, S, SP, D, FF), ou...  170 us
    unnamed x16, local copies, waits for them, and re-layouts  8 us

profile of v2, /device:TPU:0, one launch (start us, length us, event | category | flops | bytes accessed | tf_op | source)
XLA Modules:
  0.0 181.9 jit_solution(10924709493183522420)
XLA Ops:
  0.6 1.3 fusion.3.refs_7_
  1.9 169.6 %shard_map.152 = (bf16[36,77,512]{2,1,0:T(8,128)(2,1)}, bf16[36,77,512]{2,1,0:T(8,128)(2,1)}, f32[192,128]{1,0:T(8,128)}, f32[64,128]{1,0:T(8,128)}, f32[256,128...) custom-call(bf16[36,77,512]{2,1,0:T(8,128)(2,1)} %refs_0_.1, s32[36,77]{1,0:T(8,128)} %refs_1_.1, ...), custom_call_target="tpu_custom_call" | custom-call | tf_op jit(solution)/shard_map/pallas_call | solution.py:573
  171.5 1.2 slice_bitcast_fusion
  172.7 1.2 slice_bitcast_fusion.1
  173.9 0.0 copy-start
  173.9 3.8 %copy.23 = bf16[36,77,512]{2,1,0:T(8,128)(2,1)} copy(bf16[36,77,512]{2,1,0:T(8,128)(2,1)} %get-tuple-element.30) | data formatting | bytes 5677056
  177.7 0.0 copy-done
  177.7 0.0 copy-start.3
  177.7 0.0 copy-start.4
  177.7 0.0 copy-start.2
  177.7 0.0 copy-start.1
  177.7 1.6 copy.24
  179.3 0.0 copy-done.3
  179.3 0.6 copy.25
  180.0 0.0 copy-done.4
  180.0 0.6 copy.26
  180.6 0.0 copy-done.2
  180.6 0.7 copy.27
  181.3 0.0 copy-done.1
  181.3 0.7 copy.28
Async XLA Ops:
  173.9 3.8 %copy-start = (bf16[36,77,512]{2,1,0:T(8,128)(2,1)S(1)}, bf16[36,77,512]{2,1,0:T(8,128)(2,1)}, u32[]{:S(2)}) copy-start(bf16[36,77,512]{2,1,0:T(8,128)(2,1)} %get-tuple-element.31) | copy-start | bytes 8515588
  177.7 1.6 copy-start.3
  177.7 2.3 %copy-start.4 = (f32[64,128]{1,0:T(8,128)S(1)}, f32[64,128]{1,0:T(8,128)}, u32[]{:S(2)}) copy-start(f32[64,128]{1,0:T(8,128)} %get-tuple-element.18) | copy-start | bytes 98308
  177.7 2.9 %copy-start.2 = (f32[256,128]{1,0:T(8,128)S(1)}, f32[256,128]{1,0:T(8,128)}, u32[]{:S(2)}) copy-start(f32[256,128]{1,0:T(8,128)} %get-tuple-element.19) | copy-start | bytes 393220
  177.7 3.6 %copy-start.1 = (f32[256,128]{1,0:T(8,128)S(1)}, f32[256,128]{1,0:T(8,128)}, u32[]{:S(2)}) copy-start(f32[256,128]{1,0:T(8,128)} %get-tuple-element.21) | copy-start | bytes 393220
